TPU v7x, 32 devices: a whole 2x2x4 slice. The times are simulated.
32 devices in a mesh: group: 2 (over x), row: 16 (over z, y, core).
Axes of the slice: x: 2, y: 2, z: 4, core: 2. Of those that a mesh axis runs over, the one named last changes fastest.
Arguments:
- pair_act: bfloat16 [1024, 512, 128], P(('group', 'row')), parts along dimension 0, may hold values from -6 to 6
- res_mask: int32 [1024], P('group'), parts along dimension 0, may hold values 0 or 1
- w_left: bfloat16 [128, 256], replicated, may hold values from -0.5 to 0.5
- w_right: bfloat16 [128, 256], replicated, may hold values from -0.5 to 0.5
- w_gate: bfloat16 [128, 128], replicated, may hold values from -0.5 to 0.5
- w_out: bfloat16 [128, 128], replicated, may hold values from -0.5 to 0.5
Outputs:
- update: bfloat16 [1024, 512, 128], P(('group', 'row')), parts along dimension 0
There are 2 independent parts, one for each index of `group`. A program takes and returns all parts, laid end to end along the dimension named above; an argument that names none is the same for every part. Nothing has to cross between parts.
All inputs are finite; a program needn't handle non-finite values.
Results may differ from a plain program's by a relative error of at most 0.0082.
Values may be sent and summed in bfloat16 or wider, within the bound.
A program may use at most 192 MiB of HBM per device.

v0:
```python
import jax
import jax.numpy as jnp
from jax import lax
from jax.sharding import PartitionSpec as P

EPS = 1e-05


def layer_norm(values, axis):
    average = jnp.mean(values, axis=axis, keepdims=True)
    centred = values - average
    variance = jnp.mean(centred * centred, axis=axis, keepdims=True)
    return centred * lax.rsqrt(variance + EPS)


def body(pair_act, res_mask, w_left, w_right, w_gate, w_out):
    rows = pair_act.shape[0]
    width = w_left.shape[1] // 2
    first = lax.axis_index("row") * rows
    mask_rows = lax.dynamic_slice_in_dim(res_mask, first, rows)
    masks = (
        mask_rows.astype(jnp.float32)[None, :, None] * res_mask.astype(jnp.float32)[None, None, :]
    )
    normed = layer_norm(pair_act.astype(jnp.float32), 2).astype(jnp.bfloat16)

    def gated_side(weight):
        hidden = jnp.einsum("rnd,de->ern", normed, weight, preferred_element_type=jnp.float32)
        return (jax.nn.sigmoid(hidden[:width]) * hidden[width:] * masks).astype(jnp.bfloat16)

    left_edges = gated_side(w_left)
    right_edges = gated_side(w_right)
    left_cols, right_cols = (
        lax.all_to_all(left_edges, "row", split_axis=0, concat_axis=1, tiled=True),
        lax.all_to_all(right_edges, "row", split_axis=0, concat_axis=1, tiled=True),
    )
    tri_cols = jnp.einsum(
        "cik,cjk->cij", left_cols, right_cols, preferred_element_type=jnp.float32
    ).astype(jnp.bfloat16)
    tri_rows = lax.all_to_all(tri_cols, "row", split_axis=1, concat_axis=0, tiled=True)
    gates = jax.nn.sigmoid(
        jnp.einsum("rnd,de->rne", normed, w_gate, preferred_element_type=jnp.float32)
    )
    tri_normed = layer_norm(tri_rows.astype(jnp.float32), 0).astype(jnp.bfloat16)
    projected = jnp.einsum("crn,cd->rnd", tri_normed, w_out, preferred_element_type=jnp.float32)
    return (gates * projected).astype(jnp.bfloat16)


def solution(mesh):
    placed = (P(("group", "row"), None, None), P("group"), P(), P(), P(), P())
    return jax.shard_map(
        body, mesh=mesh, in_specs=placed, out_specs=P(("group", "row"), None, None), check_vma=False
    )
```

profile of v0, /device:TPU:7, one launch (start us, length us, event | category | flops | bytes accessed | tf_op | source)
XLA Modules:
  0.0 369.6 jit_solution(625389748535824809)
XLA Ops:
  0.0 0.7 convert_element_type.48
  0.7 0.9 dynamic-slice_convert_fusion
  1.6 3.6 convert_reduce_fusion
  5.2 6.0 %fusion.2 = f32[32,512]{1,0:T(8,128)S(1)} fusion(bf16[32,512,128]{2,1,0:T(8,128)(2,1)} %param.6, f32[32,512]{1,0:T(8,128)S(1)} %broadcast_multiply_fusion.2), kind=kLoop, calls=%fused_computation.6 | loop fusion | flops 8372224 | bytes 4325376 | tf_op jit(solution)/shard_map/reduce_sum | solution.py:12
  11.3 0.0 copy-start.5
  11.3 7.6 %convolution_bitcast_fusion.1 = f32[256,32,512]{0,2,1:T(8,128)S(1)} fusion(bf16[32,512,128]{2,1,0:T(8,128)(2,1)S(1)} %copy-done.2, f32[32,512]{1,0:T(8,128)S(1)} %add_rsqrt_fusion.1, f32[32,512]{1,0:T(8,128)S(1)} %broadcast_multiply_fusion.2, bf16[128,256]{1,0:T(8,128)(2,1)S(1)} %copy-done), kind=kOutput, calls=%fused_computation.5 | convolution fusion | flops 1082130432 | bytes 21168128 | tf_op jit(solution)/shard_map/rnd,de->ern/dot_general | solution.py:27
  18.9 9.0 %convolution_bitcast_fusion = f32[256,32,512]{0,2,1:T(8,128)} fusion(bf16[32,512,128]{2,1,0:T(8,128)(2,1)S(1)} %copy-done.2, f32[32,512]{1,0:T(8,128)S(1)} %add_rsqrt_fusion.1, f32[32,512]{1,0:T(8,128)S(1)} %broadcast_multiply_fusion.2, bf16[128,256]{1,0:T(8,128)(2,1)S(1)} %copy-done.5), kind=kOutput, calls=%fused_computation.4 | convolution fusion | flops 1082130432 | bytes 21168128 | tf_op jit(solution)/shard_map/rnd,de->ern/dot_general | solution.py:27
  27.9 0.1 broadcast_multiply_fusion
  28.0 12.1 %fusion.5 = (bf16[128,32,512]{0,2,1:T(8,128)(2,1)}, bf16[128,32,512]{0,2,1:T(8,128)(2,1)}) fusion(f32[256,32,512]{0,2,1:T(8,128)} %convolution_bitcast_fusion, f32[32,512]{1,0:T(8,128)S(1)} %broadcast_multiply_fusion, f32[256,32,512]{0,2,1:T(8,128)S(1)} %convolution_bitcast_fusion.1), kind=kLoop, calls=%fused_computation.10 | loop fusion | flops 25165824 | bytes 42008576 | tf_op jit(solution)/shard_map/convert_element_type | solution.py:28
  40.1 8.0 %copy.24 = bf16[128,32,512]{2,1,0:T(8,128)(2,1)} copy(bf16[128,32,512]{0,2,1:T(8,128)(2,1)} %get-tuple-element.7) | data formatting | bytes 8388608 | tf_op jit(solution)/shard_map/convert_element_type | solution.py:28
  48.0 6.7 %all-to-all-start.1 = ((bf16[128,32,512]{2,1,0:T(8,128)(2,1)}), bf16[128,32,512]{2,1,0:T(8,128)(2,1)}, u32[]{:S(2)}, u32[]{:S(2)}) async-start(bf16[128,32,512]{2,1,0:T(8,128)(2,1)} %copy.24), calls=%async_computation.1 | async-start | bytes 8388608 | tf_op jit(solution)/shard_map/all_to_all | solution.py:34
  54.7 7.8 %copy.22 = bf16[128,32,512]{2,1,0:T(8,128)(2,1)} copy(bf16[128,32,512]{0,2,1:T(8,128)(2,1)} %get-tuple-element.8) | data formatting | bytes 8388608 | tf_op jit(solution)/shard_map/convert_element_type | solution.py:28
  62.5 74.8 %all-to-all-done.1 = bf16[128,32,512]{2,1,0:T(8,128)(2,1)} async-done(((bf16[128,32,512]{2,1,0:T(8,128)(2,1)}), bf16[128,32,512]{2,1,0:T(8,128)(2,1)}, u32[]{:S(2)}, u32[]{:S(2)}) %all-to-all-start.1) | async-done | bytes 4194336 | tf_op jit(solution)/shard_map/all_to_all | solution.py:34
  137.3 14.8 %all-to-all-start = ((bf16[128,32,512]{2,1,0:T(8,128)(2,1)}), bf16[128,32,512]{2,1,0:T(8,128)(2,1)}, u32[]{:S(2)}, u32[]{:S(2)}) async-start(bf16[128,32,512]{2,1,0:T(8,128)(2,1)} %copy.22), calls=%async_computation | async-start | bytes 8388608 | tf_op jit(solution)/shard_map/all_to_all | solution.py:33
  152.1 4.7 %copy.25 = bf16[8,16,32,512]{3,2,1,0:T(8,128)(2,1)} copy(bf16[8,16,32,512]{3,2,0,1:T(8,128)(2,1)} %bitcast.9) | data formatting | bytes 8388608 | tf_op jit(solution)/shard_map/all_to_all | solution.py:34
  156.8 77.9 %all-to-all-done = bf16[128,32,512]{2,1,0:T(8,128)(2,1)} async-done(((bf16[128,32,512]{2,1,0:T(8,128)(2,1)}), bf16[128,32,512]{2,1,0:T(8,128)(2,1)}, u32[]{:S(2)}, u32[]{:S(2)}) %all-to-all-start) | async-done | bytes 4194336 | tf_op jit(solution)/shard_map/all_to_all | solution.py:33
  234.7 2.7 copy.23
  237.4 0.7 copy-done.4
  238.1 2.4 convolution_convert_fusion
  240.5 2.4 copy.26
  242.9 106.8 %all_to_all.45 = bf16[8,512,512]{2,0,1:T(8,128)(2,1)S(1)} all-to-all(bf16[8,512,512]{2,0,1:T(8,128)(2,1)S(1)} %copy.26), channel_id=1, replica_groups=mesh['group'=2,'row'=16] {'row'}, dimensions={1} | all-to-all | bytes 8388608 | tf_op jit(solution)/shard_map/all_to_all | solution.py:39
  349.7 1.7 fusion.26
  351.4 0.7 fusion.16
  352.1 1.1 multiply_reduce_fusion
  353.3 1.9 copy.28
  355.1 0.0 copy-start.6
  355.2 2.4 fusion.15
  357.6 0.0 copy-start.3
  357.6 0.0 copy-start.7
  357.6 4.9 %fusion.17 = f32[32,512,128]{2,1,0:T(8,128)S(1)} fusion(bf16[128,32,512]{2,1,0:T(8,128)(2,1)S(1)} %fusion.15, bf16[128,128]{1,0:T(8,128)(2,1)S(1)} %copy-done.6), kind=kOutput, calls=%fused_computation.29 | convolution fusion | flops 536870912 | bytes 12615680 | tf_op jit(solution)/shard_map/crn,cd->rnd/dot_general | solution.py:44
  362.5 0.0 copy-start.1
  362.5 7.0 %multiply_convert_fusion = bf16[32,512,128]{2,1,0:T(8,128)(2,1)} fusion(f32[32,512,128]{2,1,0:T(8,128)S(1)} %fusion.17, bf16[32,512,128]{2,1,0:T(8,128)(2,1)S(1)} %copy-done.3, f32[32,512]{1,0:T(8,128)S(1)} %add_rsqrt_fusion.1, f32[32,512]{1,0:T(8,128)S(1)} %broadcast_multiply_fusion.2, bf16[128,128]{1,0:T(8,128)(2,1)S(1)} %copy-done.7), kind=kOutput, calls=%fused_computation.26 | convolution fusion | flops 555745280 | bytes 16941056 | tf_op jit(solution)/shard_map/rnd,de->rne/dot_general | solution.py:41
  (14 shorter events, 0.1 us)
Async XLA Ops:
  0.0 11.3 %copy-start = (bf16[128,256]{1,0:T(8,128)(2,1)S(1)}, bf16[128,256]{1,0:T(8,128)(2,1)}, u32[]{:S(2)}) copy-start(bf16[128,256]{1,0:T(8,128)(2,1)} %param.8) | copy-start | bytes 196612
  0.7 10.5 %copy-start.2 = (bf16[32,512,128]{2,1,0:T(8,128)(2,1)S(1)}, bf16[32,512,128]{2,1,0:T(8,128)(2,1)}, u32[]{:S(2)}) copy-start(bf16[32,512,128]{2,1,0:T(8,128)(2,1)} %param.6) | copy-start | bytes 12582916
  11.3 7.7 %copy-start.5 = (bf16[128,256]{1,0:T(8,128)(2,1)S(1)}, bf16[128,256]{1,0:T(8,128)(2,1)}, u32[]{:S(2)}) copy-start(bf16[128,256]{1,0:T(8,128)(2,1)} %param.9) | copy-start | bytes 196612
  48.0 89.3 %all-to-all-start.1 = ((bf16[128,32,512]{2,1,0:T(8,128)(2,1)}), bf16[128,32,512]{2,1,0:T(8,128)(2,1)}, u32[]{:S(2)}, u32[]{:S(2)}) async-start(bf16[128,32,512]{2,1,0:T(8,128)(2,1)} %copy.24), calls=%async_computation.1 | async-start | bytes 8388608 | tf_op jit(solution)/shard_map/all_to_all | solution.py:34
  137.3 97.4 %all-to-all-start = ((bf16[128,32,512]{2,1,0:T(8,128)(2,1)}), bf16[128,32,512]{2,1,0:T(8,128)(2,1)}, u32[]{:S(2)}, u32[]{:S(2)}) async-start(bf16[128,32,512]{2,1,0:T(8,128)(2,1)} %copy.22), calls=%async_computation | async-start | bytes 8388608 | tf_op jit(solution)/shard_map/all_to_all | solution.py:33
  234.7 3.4 copy-start.4
  355.1 2.4 copy-start.6
  357.6 4.9 %copy-start.3 = (bf16[32,512,128]{2,1,0:T(8,128)(2,1)S(1)}, bf16[32,512,128]{2,1,0:T(8,128)(2,1)}, u32[]{:S(2)}) copy-start(bf16[32,512,128]{2,1,0:T(8,128)(2,1)} %param.6) | copy-start | bytes 12582916
  357.6 4.9 %copy-start.7 = (bf16[128,128]{1,0:T(8,128)(2,1)S(1)}, bf16[128,128]{1,0:T(8,128)(2,1)}, u32[]{:S(2)}) copy-start(bf16[128,128]{1,0:T(8,128)(2,1)} %param.10) | copy-start | bytes 98308
  362.5 7.0 %copy-start.1 = (bf16[128,256]{1,0:T(8,128)(2,1)S(1)}, bf16[128,256]{1,0:T(8,128)(2,1)}, u32[]{:S(2)}) copy-start(bf16[128,256]{1,0:T(8,128)(2,1)} %param.8) | copy-start | bytes 196612
where the time goes:
time: 371 us; the launch traced here: 370 us
  waiting for transfers between devices  153 us (41%)
  blocking collectives  107 us (29%)
  matrix products  30.9 us (8%)
  other arithmetic  29.4 us (8%)
  local copies, waits for them, and re-layouts  28.2 us (8%)
  starting transfers between devices  21.4 us (6%)
    all_to_all x1, blocking collectives, body(): lax.all_to_all(tri_cols, 'row', split_axis=1, concat_axis=0, tiled=True)  107 us
    all_to_all x1, waiting for transfers between devices, body(): lax.all_to_all(left_edges, 'row', split_axis=0, concat_axis=1, tiled=True)  77.9 us
    all_to_all x1, waiting for transfers between devices, body(): lax.all_to_all(right_edges, 'row', split_axis=0, concat_axis=1, tiled=True)  74.8 us
    dot_general x2, matrix products, gated_side(): jnp.einsum('rnd,de->ern', normed, weight, preferred_element_type=jnp.floa...  16.6 us
    convert_element_type x2, local copies, waits for them, and re-layouts, gated_side(): (jax.nn.sigmoid(hidden[:width]) * hidden[width:] * masks).astype(jnp.bflo...  15.8 us
    all_to_all x1, starting transfers between devices, body(): lax.all_to_all(left_edges, 'row', split_axis=0, concat_axis=1, tiled=True)  14.8 us
    convert_element_type x1, other arithmetic, gated_side(): (jax.nn.sigmoid(hidden[:width]) * hidden[width:] * masks).astype(jnp.bflo...  12.1 us
  transfers between devices with their start and end apart: 2, of which 2 were waited for; matrix products, arithmetic and copies ran while one was open for 3% of the time, Pallas kernels for 0%

commit v1 on v0

--- a/solution.py
+++ b/solution.py
@@ -1,9 +1,18 @@
+import functools
+
 import jax
 import jax.numpy as jnp
 from jax import lax
+from jax.experimental import pallas as pl
+from jax.experimental.pallas import tpu as pltpu
 from jax.sharding import PartitionSpec as P
 
 EPS = 1e-05
+TILE = 16
+LANES = 128
+HALVES = 2
+PITCH = 136
+FPITCH = 24
 
 
 def layer_norm(values, axis):
@@ -13,7 +22,11 @@
     return centred * lax.rsqrt(variance + EPS)
 
 
-def body(pair_act, res_mask, w_left, w_right, w_gate, w_out):
+def sigmoid(x):
+    return 0.5 + 0.5 * jnp.tanh(0.5 * x)
+
+
+def plain_body(pair_act, res_mask, w_left, w_right, w_gate, w_out):
     rows = pair_act.shape[0]
     width = w_left.shape[1] // 2
     first = lax.axis_index("row") * rows
@@ -45,8 +58,226 @@
     return (gates * projected).astype(jnp.bfloat16)
 
 
+def kernel(
+    n, pair, mask_s, mask_v, wt, w_gate, w_out, out,
+    normed, own_l, own_r, got_l, got_r, tri, got_t, stage, turn,
+    sem_l, sem_r, sem_t, out_l, out_r, out_t,
+):
+    rows, _, blocks, _, _ = pair.shape
+    width = own_l.shape[0]
+    length = own_l.shape[2]
+    peers = n // HALVES
+    share = width // peers
+    lane_tiles = length // LANES
+    block_devs = LANES // (TILE * blocks)
+    me = lax.axis_index("row")
+    half = me // peers
+    spot = lax.rem(me, peers)
+
+    barrier = pltpu.get_barrier_semaphore()
+    for step in range(1, n):
+        pl.semaphore_signal(barrier, inc=1, device_id={"row": lax.rem(me + step, n)})
+    pl.semaphore_wait(barrier, n - 1)
+
+    def remote(src, dst, send, recv, device):
+        pltpu.make_async_remote_copy(
+            src_ref=src, dst_ref=dst, send_sem=send, recv_sem=recv, device_id={"row": device}
+        ).start()
+
+    def edges(block):
+        def one_row(r, carry):
+            row = block * TILE + r
+            mask_i = mask_s[me * rows + row].astype(jnp.float32)
+            for kt in range(lane_tiles):
+                devs = pl.ds(kt * block_devs, block_devs)
+                x = pair[row, devs].reshape(LANES, -1).astype(jnp.float32)
+                nrm = layer_norm(x, 1).astype(jnp.bfloat16)
+                normed[row, devs] = nrm.reshape(block_devs, blocks, TILE, -1)
+                h = lax.dot_general(
+                    wt[...], nrm, (((1,), (1,)), ((), ())), preferred_element_type=jnp.float32
+                )
+                mask_k = mask_v[:, kt * LANES : (kt + 1) * LANES].astype(jnp.float32) * mask_i
+                for side in range(2):
+                    gate = h[side * 2 * width : (side * 2 + 1) * width]
+                    value = h[(side * 2 + 1) * width : (side * 2 + 2) * width]
+                    stage[kt, side, pl.ds(r * PITCH, width), :] = sigmoid(gate) * value * mask_k
+            return carry
+
+        lax.fori_loop(0, TILE, one_row, 0)
+
+        def one_channel(c, carry):
+            for side, own in enumerate((own_l, own_r)):
+                for kt in range(lane_tiles):
+                    v = stage[kt, side, pl.ds(c, TILE, stride=PITCH), :]
+                    own[c, block * TILE : (block + 1) * TILE, kt * LANES : (kt + 1) * LANES] = (
+                        v.astype(jnp.bfloat16)
+                    )
+            return carry
+
+        lax.fori_loop(0, width, one_channel, 0, unroll=4)
+
+    def piece(ref, at, block):
+        return ref.at[pl.ds(at * share, share), pl.ds(block * TILE, TILE)]
+
+    def send_edges(block):
+        for step in range(peers):
+            to = lax.rem(spot + step, peers)
+            remote(
+                piece(own_r, to, block), got_r.at[block, 1, :, pl.ds(spot * TILE, TILE)],
+                out_r.at[block], sem_r.at[block, 1], (1 - half) * peers + to,
+            )
+        l_dst = got_l.at[:, pl.ds(spot * rows + block * TILE, TILE)]
+        r_dst = got_r.at[block, 0, :, pl.ds(spot * TILE, TILE)]
+        for step in range(1, peers):
+            to = lax.rem(spot + step, peers)
+            remote(piece(own_l, to, block), l_dst, out_l, sem_l, half * peers + to)
+            remote(
+                piece(own_r, to, block), r_dst, out_r.at[block], sem_r.at[block, 0],
+                half * peers + to,
+            )
+        pltpu.make_async_copy(piece(own_l, spot, block), l_dst, sem_l).start()
+        pltpu.make_async_copy(piece(own_r, spot, block), r_dst, sem_r.at[block, 0]).start()
+
+    def contract(block, rel):
+        pltpu.make_async_copy(
+            got_r.at[block, rel], got_r.at[block, rel], sem_r.at[block, rel]
+        ).wait()
+
+        def one(c, carry):
+            tri[block, rel, c] = lax.dot_general(
+                got_l[c], got_r[block, rel, c], (((1,), (1,)), ((), ())),
+                preferred_element_type=jnp.float32,
+            ).astype(jnp.bfloat16)
+            return carry
+
+        lax.fori_loop(0, share, one, 0)
+        dst = got_t.at[block, rel, pl.ds(spot * share, share)]
+        for step in range(1, peers):
+            to = lax.rem(spot + step, peers)
+            remote(
+                tri.at[block, rel, :, pl.ds(to * rows, rows)], dst,
+                out_t.at[block, rel], sem_t.at[block, rel], half * peers + to,
+            )
+        pltpu.make_async_copy(
+            tri.at[block, rel, :, pl.ds(spot * rows, rows)], dst, sem_t.at[block, rel]
+        ).start()
+
+    def finish(block, rel):
+        pltpu.make_async_copy(
+            got_t.at[block, rel], got_t.at[block, rel], sem_t.at[block, rel]
+        ).wait()
+        source = lax.rem(half + rel, HALVES)
+        devs = pl.ds(source * peers, peers)
+        for ib in range(rows // TILE):
+            i_rows = pl.ds(ib * TILE, TILE)
+
+            def load(c):
+                return got_t[block, rel, c, i_rows, :].astype(jnp.float32)
+
+            zero = jnp.zeros((TILE, peers * TILE), jnp.float32)
+            mean = lax.fori_loop(0, width, lambda c, s: s + load(c), zero, unroll=8) * (1.0 / width)
+
+            def spread(c, s):
+                d = load(c) - mean
+                return s + d * d
+
+            var = lax.fori_loop(0, width, spread, zero, unroll=8) * (1.0 / width)
+            scale = lax.rsqrt(var + EPS)
+
+            def put(c, carry):
+                turn[pl.ds(c * FPITCH, TILE), :] = (load(c) - mean) * scale
+                return carry
+
+            lax.fori_loop(0, width, put, 0, unroll=8)
+
+            def one_row(i, carry):
+                row = ib * TILE + i
+                tn = turn[pl.ds(i, width, stride=FPITCH), :].astype(jnp.bfloat16)
+                projected = lax.dot_general(
+                    tn, w_out[...], (((0,), (0,)), ((), ())), preferred_element_type=jnp.float32
+                )
+                nrm = normed[row, devs, block].reshape(peers * TILE, -1)
+                gates = sigmoid(jnp.dot(nrm, w_gate[...], preferred_element_type=jnp.float32))
+                out[row, devs, block] = (
+                    (gates * projected).astype(jnp.bfloat16).reshape(peers, TILE, -1)
+                )
+                return carry
+
+            lax.fori_loop(0, TILE, one_row, 0, unroll=2)
+
+    for block in range(blocks):
+        edges(block)
+        send_edges(block)
+    pltpu.make_async_copy(got_l, got_l, sem_l).wait()
+    steps = [(block, rel) for rel in range(HALVES) for block in range(blocks)]
+    for at, step in enumerate(steps):
+        contract(*step)
+        if at >= 1:
+            finish(*steps[at - 1])
+    finish(*steps[-1])
+
+    rest = (peers - 1) * share
+    l_sent = own_l.at[pl.ds(0, rest)]
+    pltpu.make_async_copy(l_sent, l_sent, out_l).wait()
+    for block in range(blocks):
+        both = own_r.at[pl.ds(0, width - share // 2)]
+        pltpu.make_async_copy(both, both, out_r.at[block]).wait()
+        for rel in range(HALVES):
+            t_sent = tri.at[block, rel, :, pl.ds(0, (peers - 1) * rows)]
+            pltpu.make_async_copy(t_sent, t_sent, out_t.at[block, rel]).wait()
+
+
+def fused_body(n, pair_act, res_mask, w_left, w_right, w_gate, w_out):
+    rows, length, depth = pair_act.shape
+    width = w_left.shape[1] // 2
+    peers = n // HALVES
+    share = width // peers
+    blocks = rows // TILE
+    bf16 = jnp.bfloat16
+    wt = jnp.concatenate([w_left, w_right], axis=1).T
+    view = (rows, n, blocks, TILE, depth)
+    vmem = pl.BlockSpec(memory_space=pltpu.VMEM)
+    dma = pltpu.SemaphoreType.DMA
+    result = pl.pallas_call(
+        functools.partial(kernel, n),
+        out_shape=jax.ShapeDtypeStruct(view, bf16),
+        in_specs=[vmem, pl.BlockSpec(memory_space=pltpu.SMEM)] + [vmem] * 4,
+        out_specs=vmem,
+        scratch_shapes=[
+            pltpu.VMEM(view, bf16),
+            pltpu.VMEM((width, rows, length), bf16),
+            pltpu.VMEM((width, rows, length), bf16),
+            pltpu.VMEM((share, peers * rows, length), bf16),
+            pltpu.VMEM((blocks, HALVES, share, peers * TILE, length), bf16),
+            pltpu.VMEM((blocks, HALVES, share, peers * rows, peers * TILE), bf16),
+            pltpu.VMEM((blocks, HALVES, width, rows, peers * TILE), bf16),
+            pltpu.VMEM((length // LANES, 2, TILE * PITCH, LANES), jnp.float32),
+            pltpu.VMEM((width * FPITCH, LANES), jnp.float32),
+            dma,
+            dma((blocks, HALVES)),
+            dma((blocks, HALVES)),
+            dma,
+            dma((blocks,)),
+            dma((blocks, HALVES)),
+        ],
+        compiler_params=pltpu.CompilerParams(
+            collective_id=0, has_side_effects=True, vmem_limit_bytes=62 * 2**20
+        ),
+    )(pair_act.reshape(view), res_mask, res_mask.reshape(1, length), wt, w_gate, w_out)
+    return result.reshape(rows, length, depth)
+
+
+def body(n, pair_act, *others):
+    rows, length, depth = pair_act.shape
+    fits = rows == 2 * TILE and n // HALVES * TILE == LANES and depth == LANES and length == n * rows
+    if fits and others[1].shape[1] == 2 * LANES:
+        return fused_body(n, pair_act, *others)
+    return plain_body(pair_act, *others)
+
+
 def solution(mesh):
     placed = (P(("group", "row"), None, None), P("group"), P(), P(), P(), P())
     return jax.shard_map(
-        body, mesh=mesh, in_specs=placed, out_specs=P(("group", "row"), None, None), check_vma=False
-    )
+        functools.partial(body, mesh.shape["row"]), mesh=mesh, in_specs=placed,
+        out_specs=P(("group", "row"), None, None), check_vma=False,
+    )

time: 371 us -> 279 us (0.75)
  Pallas kernels: 0 us -> 270 us
  waiting for transfers between devices: 153 us -> 0 us
  blocking collectives: 107 us -> 0 us
  matrix products: 30.9 us -> 0 us
  other arithmetic: 29.4 us -> 0.67 us
  local copies, waits for them, and re-layouts: 28.2 us -> 6.56 us
  starting transfers between devices: 21.4 us -> 0 us
    pallas_call x0 -> x1, Pallas kernels: none -> 270 us  [fused_body(): pl.pallas_call(functools.partial(kernel, n), out_shape=jax.ShapeDtypeStru...]
    all_to_all x2 -> x0, waiting for transfers between devices: 153 us -> none  [the longest x1 77.9 us: body(): lax.all_to_all(left_edges, 'row', split_axis=0, concat_axis=1, tiled=True)]
    all_to_all x1 -> x0, blocking collectives: 107 us -> none  [body(): lax.all_to_all(tri_cols, 'row', split_axis=1, concat_axis=0, tiled=True)]
    dot_general x5 -> x0, matrix products: 30.9 us -> none  [the longest x2 16.6 us: gated_side(): jnp.einsum('rnd,de->ern', normed, weight, preferred_element_type=jnp.floa...]
    all_to_all x2 -> x0, starting transfers between devices: 21.4 us -> none  [the longest x1 14.8 us: body(): lax.all_to_all(left_edges, 'row', split_axis=0, concat_axis=1, tiled=True)]
    convert_element_type x4 -> x0, local copies, waits for them, and re-layouts: 20 us -> none  [the longest x2 15.8 us: gated_side(): (jax.nn.sigmoid(hidden[:width]) * hidden[width:] * masks).astype(jnp.bflo...]
    convert_element_type x4 -> x0, other arithmetic: 16.1 us -> none  [the longest x1 12.1 us: gated_side(): (jax.nn.sigmoid(hidden[:width]) * hidden[width:] * masks).astype(jnp.bflo...]
    reduce_sum x4 -> x0, other arithmetic: 11.4 us -> none  [the longest x2 7.13 us: layer_norm(): variance = jnp.mean(centred * centred, axis=axis, keepdims=True)]
  transfers between devices with their start and end apart: 2 -> 0, of which waited for: 2 -> 0; matrix products, arithmetic and copies ran while one was open for 3% -> 0% of each run, Pallas kernels for 0% -> 0%
where the time goes in v1:
time: 279 us; the launch traced here: 277 us
  Pallas kernels  270 us (97%)
  local copies, waits for them, and re-layouts  6.56 us (2%)
    pallas_call x1, Pallas kernels, fused_body(): pl.pallas_call(functools.partial(kernel, n), out_shape=jax.ShapeDtypeStru...  270 us
    unnamed x3, local copies, waits for them, and re-layouts  6.56 us

profile of v1, /device:TPU:7, one launch (start us, length us, event | category | flops | bytes accessed | tf_op | source)
XLA Modules:
  0.0 276.9 jit_solution(12686568179598533202)
XLA Ops:
  0.0 0.9 copy.7
  1.0 1.0 copy.8
  1.9 0.7 maximum_bitcast_fusion.wt
  2.6 269.6 %shard_map.64 = bf16[32,16,2,16,128]{4,3,2,1,0:T(8,128)(2,1)} custom-call(bf16[32,16,2,16,128]{4,3,2,1,0:T(8,128)(2,1)} %bitcast.6, s32[512]{0:T(512)} %mask_s.1, s32[1,512]{1,0:T(1,128)} %bitcast.7, bf16[512,128]{1,0:T(8,128)(2,1)} %maximum_bitcast_fusion.wt, bf16[128,128]{1,0:T(8,128)(2,1)} %w_gate.1, bf16[128,128]{1,0:T(8,128)(2,1)} %w_out.1), custom_call_target="tpu_custom_call" | custom-call | tf_op jit(solution)/shard_map/pallas_call | solution.py:241
  272.2 4.7 %copy.10 = bf16[32,512,128]{2,1,0:T(8,128)(2,1)} copy(bf16[32,512,128]{2,1,0:T(8,128)(2,1)} %bitcast.5) | data formatting | bytes 8388608

commit v2 on v1

--- a/solution.py
+++ b/solution.py
@@ -58,31 +58,53 @@
     return (gates * projected).astype(jnp.bfloat16)
 
 
+def shares_of(width, peers):
+    outer = width * 3 // (4 * peers)
+    return outer, 2 * width // peers - outer
+
+
 def kernel(
     n, pair, mask_s, mask_v, wt, w_gate, w_out, out,
     normed, own_l, own_r, got_l, got_r, tri, got_t, stage, turn,
-    sem_l, sem_r, sem_t, out_l, out_r, out_t,
+    sem_l, sem_r, sem_t, out_l, out_r, out_x, out_t,
 ):
     rows, _, blocks, _, _ = pair.shape
     width = own_l.shape[0]
     length = own_l.shape[2]
     peers = n // HALVES
-    share = width // peers
+    plane = peers // 2
+    shares = shares_of(width, peers)
     lane_tiles = length // LANES
     block_devs = LANES // (TILE * blocks)
     me = lax.axis_index("row")
     half = me // peers
     spot = lax.rem(me, peers)
+    ring = lax.rem(spot + half * plane, peers)
+    role = ring // plane
+    lane = lax.rem(ring, plane)
+
+    def device(which_half, cls, at):
+        return which_half * peers + lax.rem(cls * plane + at + which_half * plane, peers)
+
+    def first_channel(cls, at):
+        return cls * plane * shares[0] + at * shares[cls]
+
+    def by_role(act):
+        for inner in range(2):
+            pl.when(role == inner)(functools.partial(act, inner))
 
     barrier = pltpu.get_barrier_semaphore()
     for step in range(1, n):
         pl.semaphore_signal(barrier, inc=1, device_id={"row": lax.rem(me + step, n)})
     pl.semaphore_wait(barrier, n - 1)
 
-    def remote(src, dst, send, recv, device):
+    def remote(src, dst, send, recv, to):
         pltpu.make_async_remote_copy(
-            src_ref=src, dst_ref=dst, send_sem=send, recv_sem=recv, device_id={"row": device}
+            src_ref=src, dst_ref=dst, send_sem=send, recv_sem=recv, device_id={"row": to}
         ).start()
+
+    def wait(ref, sem):
+        pltpu.make_async_copy(ref, ref, sem).wait()
 
     def edges(block):
         def one_row(r, carry):
@@ -116,32 +138,78 @@
 
         lax.fori_loop(0, width, one_channel, 0, unroll=4)
 
-    def piece(ref, at, block):
-        return ref.at[pl.ds(at * share, share), pl.ds(block * TILE, TILE)]
-
-    def send_edges(block):
-        for step in range(peers):
-            to = lax.rem(spot + step, peers)
+    def send_edges(block, inner):
+        sem_own = 0 if inner else 2
+        row_block = pl.ds(block * TILE, TILE)
+        l_rows = pl.ds(spot * rows + block * TILE, TILE)
+        r_rows = pl.ds(spot * TILE, TILE)
+
+        def targets(cls):
+            for step in range(plane):
+                at = lax.rem(lane + step, plane)
+                local = cls == inner and step == 0
+                yield at, local, pl.ds(first_channel(cls, at), shares[cls])
+
+        def cross(cls):
+            for at, _, channels in targets(cls):
+                remote(
+                    own_r.at[channels, row_block], got_r.at[block, 1, pl.ds(0, shares[cls]), r_rows],
+                    out_r.at[block], sem_r.at[block, 1], device(1 - half, cls, at),
+                )
+
+        def own_right(cls):
+            dst = got_r.at[block, 0, pl.ds(0, shares[cls]), r_rows]
+            for at, local, channels in targets(cls):
+                src = own_r.at[channels, row_block]
+                if local:
+                    pltpu.make_async_copy(src, dst, sem_r.at[block, sem_own]).start()
+                else:
+                    remote(
+                        src, dst, out_r.at[block], sem_r.at[block, sem_own], device(half, cls, at)
+                    )
+
+        def own_left(cls):
+            dst = got_l.at[pl.ds(0, shares[cls]), l_rows]
+            for at, local, channels in targets(cls):
+                src = own_l.at[channels, row_block]
+                if local:
+                    pltpu.make_async_copy(src, dst, sem_l).start()
+                else:
+                    remote(src, dst, out_l, sem_l, device(half, cls, at))
+
+        if inner:
+            cross(1)
+            cross(0)
+            own_right(0)
+            own_right(1)
+        else:
+            own_right(1)
+            cross(0)
+            own_right(0)
+        own_left(0)
+        own_left(1)
+
+    def forward(block, inner):
+        if inner:
+            part = got_r.at[
+                block, 0, pl.ds(0, shares[1]), pl.ds(half * plane * TILE, plane * TILE)
+            ]
+            wait(part, sem_r.at[block, 2])
             remote(
-                piece(own_r, to, block), got_r.at[block, 1, :, pl.ds(spot * TILE, TILE)],
-                out_r.at[block], sem_r.at[block, 1], (1 - half) * peers + to,
+                part,
+                got_r.at[block, 1, pl.ds(0, shares[1]), pl.ds(half * plane * TILE, plane * TILE)],
+                out_x.at[block], sem_r.at[block, 1], device(1 - half, 1, lane),
             )
-        l_dst = got_l.at[:, pl.ds(spot * rows + block * TILE, TILE)]
-        r_dst = got_r.at[block, 0, :, pl.ds(spot * TILE, TILE)]
-        for step in range(1, peers):
-            to = lax.rem(spot + step, peers)
-            remote(piece(own_l, to, block), l_dst, out_l, sem_l, half * peers + to)
-            remote(
-                piece(own_r, to, block), r_dst, out_r.at[block], sem_r.at[block, 0],
-                half * peers + to,
-            )
-        pltpu.make_async_copy(piece(own_l, spot, block), l_dst, sem_l).start()
-        pltpu.make_async_copy(piece(own_r, spot, block), r_dst, sem_r.at[block, 0]).start()
-
-    def contract(block, rel):
-        pltpu.make_async_copy(
-            got_r.at[block, rel], got_r.at[block, rel], sem_r.at[block, rel]
-        ).wait()
+
+    def contract(block, rel, inner):
+        share = shares[inner]
+        if rel:
+            wait(got_r.at[block, 1, pl.ds(0, share)], sem_r.at[block, 1])
+        else:
+            part = got_r.at[block, 0, pl.ds(0, share), pl.ds(0, plane * TILE)]
+            wait(part, sem_r.at[block, 0])
+            if not inner:
+                wait(part, sem_r.at[block, 2])
 
         def one(c, carry):
             tri[block, rel, c] = lax.dot_general(
@@ -151,15 +219,16 @@
             return carry
 
         lax.fori_loop(0, share, one, 0)
-        dst = got_t.at[block, rel, pl.ds(spot * share, share)]
+        dst = got_t.at[block, rel, pl.ds(first_channel(inner, lane), share)]
         for step in range(1, peers):
             to = lax.rem(spot + step, peers)
             remote(
-                tri.at[block, rel, :, pl.ds(to * rows, rows)], dst,
+                tri.at[block, rel, pl.ds(0, share), pl.ds(to * rows, rows)], dst,
                 out_t.at[block, rel], sem_t.at[block, rel], half * peers + to,
             )
         pltpu.make_async_copy(
-            tri.at[block, rel, :, pl.ds(spot * rows, rows)], dst, sem_t.at[block, rel]
+            tri.at[block, rel, pl.ds(0, share), pl.ds(spot * rows, rows)], dst,
+            sem_t.at[block, rel],
         ).start()
 
     def finish(block, rel):
@@ -207,31 +276,43 @@
 
     for block in range(blocks):
         edges(block)
-        send_edges(block)
-    pltpu.make_async_copy(got_l, got_l, sem_l).wait()
+        by_role(functools.partial(send_edges, block))
+
+    def ready(inner):
+        for block in range(blocks):
+            forward(block, inner)
+        wait(got_l.at[pl.ds(0, shares[inner])], sem_l)
+
+    by_role(ready)
     steps = [(block, rel) for rel in range(HALVES) for block in range(blocks)]
     for at, step in enumerate(steps):
-        contract(*step)
+        by_role(functools.partial(contract, *step))
         if at >= 1:
             finish(*steps[at - 1])
     finish(*steps[-1])
 
-    rest = (peers - 1) * share
-    l_sent = own_l.at[pl.ds(0, rest)]
-    pltpu.make_async_copy(l_sent, l_sent, out_l).wait()
-    for block in range(blocks):
-        both = own_r.at[pl.ds(0, width - share // 2)]
-        pltpu.make_async_copy(both, both, out_r.at[block]).wait()
-        for rel in range(HALVES):
-            t_sent = tri.at[block, rel, :, pl.ds(0, (peers - 1) * rows)]
-            pltpu.make_async_copy(t_sent, t_sent, out_t.at[block, rel]).wait()
+    def drain(inner):
+        near = width - shares[inner]
+        far = width if inner else plane * shares[0]
+        wait(own_l.at[pl.ds(0, near)], out_l)
+        for block in range(blocks):
+            wait(own_r.at[pl.ds(0, (near + far) // 2)], out_r.at[block])
+            if inner:
+                wait(got_r.at[block, 0, pl.ds(0, shares[1]), pl.ds(0, plane * TILE)], out_x.at[block])
+            for rel in range(HALVES):
+                wait(
+                    tri.at[block, rel, pl.ds(0, shares[inner]), pl.ds(0, (peers - 1) * rows)],
+                    out_t.at[block, rel],
+                )
+
+    by_role(drain)
 
 
 def fused_body(n, pair_act, res_mask, w_left, w_right, w_gate, w_out):
     rows, length, depth = pair_act.shape
     width = w_left.shape[1] // 2
     peers = n // HALVES
-    share = width // peers
+    share = max(shares_of(width, peers))
     blocks = rows // TILE
     bf16 = jnp.bfloat16
     wt = jnp.concatenate([w_left, w_right], axis=1).T
@@ -254,9 +335,10 @@
             pltpu.VMEM((length // LANES, 2, TILE * PITCH, LANES), jnp.float32),
             pltpu.VMEM((width * FPITCH, LANES), jnp.float32),
             dma,
-            dma((blocks, HALVES)),
+            dma((blocks, 3)),
             dma((blocks, HALVES)),
             dma,
+            dma((blocks,)),
             dma((blocks,)),
             dma((blocks, HALVES)),
         ],

time: 279 us -> 249 us (0.89)
  Pallas kernels: 270 us -> 242 us
    pallas_call x1, Pallas kernels: 270 us -> 242 us  [fused_body(): pl.pallas_call(functools.partial(kernel, n), out_shape=jax.ShapeDtypeStru...]
where the time goes in v2:
time: 249 us
  Pallas kernels  242 us (97%)
  local copies, waits for them, and re-layouts  6.56 us (3%)
    pallas_call x1, Pallas kernels, fused_body(): pl.pallas_call(functools.partial(kernel, n), out_shape=jax.ShapeDtypeStru...  242 us
    unnamed x3, local copies, waits for them, and re-layouts  6.56 us

profile of v2, /device:TPU:7, one launch (start us, length us, event | category | flops | bytes accessed | tf_op | source)
XLA Modules:
  0.0 249.0 jit_solution(4480499679627973556)
XLA Ops:
  0.0 0.9 copy.7
  1.0 1.0 copy.8
  1.9 0.7 maximum_bitcast_fusion.wt
  2.6 241.7 %shard_map.64 = bf16[32,16,2,16,128]{4,3,2,1,0:T(8,128)(2,1)} custom-call(bf16[32,16,2,16,128]{4,3,2,1,0:T(8,128)(2,1)} %bitcast.6, s32[512]{0:T(512)} %mask_s.1, s32[1,512]{1,0:T(1,128)} %bitcast.7, bf16[512,128]{1,0:T(8,128)(2,1)} %maximum_bitcast_fusion.wt, bf16[128,128]{1,0:T(8,128)(2,1)} %w_gate.1, bf16[128,128]{1,0:T(8,128)(2,1)} %w_out.1), custom_call_target="tpu_custom_call" | custom-call | tf_op jit(solution)/shard_map/pallas_call | solution.py:322
  244.3 4.7 %copy.10 = bf16[32,512,128]{2,1,0:T(8,128)(2,1)} copy(bf16[32,512,128]{2,1,0:T(8,128)(2,1)} %bitcast.5) | data formatting | bytes 8388608

commit v3 on v2

--- a/solution.py
+++ b/solution.py
@@ -13,6 +13,7 @@
 HALVES = 2
 PITCH = 136
 FPITCH = 24
+GROUPS = 4
 
 
 def layer_norm(values, axis):
@@ -64,9 +65,9 @@
 
 
 def kernel(
-    n, pair, mask_s, mask_v, wt, w_gate, w_out, out,
-    normed, own_l, own_r, got_l, got_r, tri, got_t, stage, turn,
-    sem_l, sem_r, sem_t, out_l, out_r, out_x, out_t,
+    n, pair, mask_s, mask_v, w_left, w_right, w_gate, w_out, result,
+    normed, own_l, own_r, got_l, got_r, tri, got_t, stage, turn, wt, out,
+    sem_l, sem_r, sem_c, sem_t, out_l, out_r, out_x, out_t, sem_out,
 ):
     rows, _, blocks, _, _ = pair.shape
     width = own_l.shape[0]
@@ -96,7 +97,8 @@
     barrier = pltpu.get_barrier_semaphore()
     for step in range(1, n):
         pl.semaphore_signal(barrier, inc=1, device_id={"row": lax.rem(me + step, n)})
-    pl.semaphore_wait(barrier, n - 1)
+    for side, weight in enumerate((w_left, w_right)):
+        wt[side] = weight[...].astype(jnp.float32).T.astype(jnp.bfloat16)
 
     def remote(src, dst, send, recv, to):
         pltpu.make_async_remote_copy(
@@ -106,39 +108,40 @@
     def wait(ref, sem):
         pltpu.make_async_copy(ref, ref, sem).wait()
 
-    def edges(block):
+    def edges(block, side):
+        own = own_r if side else own_l
+
         def one_row(r, carry):
             row = block * TILE + r
             mask_i = mask_s[me * rows + row].astype(jnp.float32)
             for kt in range(lane_tiles):
                 devs = pl.ds(kt * block_devs, block_devs)
-                x = pair[row, devs].reshape(LANES, -1).astype(jnp.float32)
-                nrm = layer_norm(x, 1).astype(jnp.bfloat16)
-                normed[row, devs] = nrm.reshape(block_devs, blocks, TILE, -1)
+                if side:
+                    x = pair[row, devs].reshape(LANES, -1).astype(jnp.float32)
+                    nrm = layer_norm(x, 1).astype(jnp.bfloat16)
+                    normed[row, devs] = nrm.reshape(block_devs, blocks, TILE, -1)
+                else:
+                    nrm = normed[row, devs].reshape(LANES, -1)
                 h = lax.dot_general(
-                    wt[...], nrm, (((1,), (1,)), ((), ())), preferred_element_type=jnp.float32
+                    wt[side], nrm, (((1,), (1,)), ((), ())), preferred_element_type=jnp.float32
                 )
                 mask_k = mask_v[:, kt * LANES : (kt + 1) * LANES].astype(jnp.float32) * mask_i
-                for side in range(2):
-                    gate = h[side * 2 * width : (side * 2 + 1) * width]
-                    value = h[(side * 2 + 1) * width : (side * 2 + 2) * width]
-                    stage[kt, side, pl.ds(r * PITCH, width), :] = sigmoid(gate) * value * mask_k
+                stage[kt, pl.ds(r * PITCH, width), :] = sigmoid(h[:width]) * h[width:] * mask_k
             return carry
 
         lax.fori_loop(0, TILE, one_row, 0)
 
         def one_channel(c, carry):
-            for side, own in enumerate((own_l, own_r)):
-                for kt in range(lane_tiles):
-                    v = stage[kt, side, pl.ds(c, TILE, stride=PITCH), :]
-                    own[c, block * TILE : (block + 1) * TILE, kt * LANES : (kt + 1) * LANES] = (
-                        v.astype(jnp.bfloat16)
-                    )
+            for kt in range(lane_tiles):
+                v = stage[kt, pl.ds(c, TILE, stride=PITCH), :]
+                own[c, block * TILE : (block + 1) * TILE, kt * LANES : (kt + 1) * LANES] = (
+                    v.astype(jnp.bfloat16)
+                )
             return carry
 
-        lax.fori_loop(0, width, one_channel, 0, unroll=4)
-
-    def send_edges(block, inner):
+        lax.fori_loop(0, width, one_channel, 0, unroll=8)
+
+    def send_edges(block, side, inner):
         sem_own = 0 if inner else 2
         row_block = pl.ds(block * TILE, TILE)
         l_rows = pl.ds(spot * rows + block * TILE, TILE)
@@ -150,12 +153,16 @@
                 local = cls == inner and step == 0
                 yield at, local, pl.ds(first_channel(cls, at), shares[cls])
 
-        def cross(cls):
-            for at, _, channels in targets(cls):
-                remote(
-                    own_r.at[channels, row_block], got_r.at[block, 1, pl.ds(0, shares[cls]), r_rows],
-                    out_r.at[block], sem_r.at[block, 1], device(1 - half, cls, at),
-                )
+        def cross(classes):
+            for group in range(GROUPS):
+                for cls in classes:
+                    part = shares[cls] // GROUPS
+                    for at, _, _ in targets(cls):
+                        remote(
+                            own_r.at[pl.ds(first_channel(cls, at) + group * part, part), row_block],
+                            got_r.at[block, 1, pl.ds(group * part, part), r_rows],
+                            out_r.at[block], sem_c.at[block, group], device(1 - half, cls, at),
+                        )
 
         def own_right(cls):
             dst = got_r.at[block, 0, pl.ds(0, shares[cls]), r_rows]
@@ -177,35 +184,36 @@
                 else:
                     remote(src, dst, out_l, sem_l, device(half, cls, at))
 
-        if inner:
-            cross(1)
-            cross(0)
+        if not side:
+            own_left(0)
+            own_left(1)
+        elif inner:
+            cross((1, 0))
             own_right(0)
             own_right(1)
         else:
             own_right(1)
-            cross(0)
+            cross((0,))
             own_right(0)
-        own_left(0)
-        own_left(1)
 
     def forward(block, inner):
         if inner:
-            part = got_r.at[
-                block, 0, pl.ds(0, shares[1]), pl.ds(half * plane * TILE, plane * TILE)
-            ]
-            wait(part, sem_r.at[block, 2])
-            remote(
-                part,
-                got_r.at[block, 1, pl.ds(0, shares[1]), pl.ds(half * plane * TILE, plane * TILE)],
-                out_x.at[block], sem_r.at[block, 1], device(1 - half, 1, lane),
-            )
+            from_ends = pl.ds(half * plane * TILE, plane * TILE)
+            wait(got_r.at[block, 0, pl.ds(0, shares[1]), from_ends], sem_r.at[block, 2])
+            part = shares[1] // GROUPS
+            for group in range(GROUPS):
+                channels = pl.ds(group * part, part)
+                remote(
+                    got_r.at[block, 0, channels, from_ends],
+                    got_r.at[block, 1, channels, from_ends],
+                    out_x.at[block], sem_c.at[block, group], device(1 - half, 1, lane),
+                )
 
     def contract(block, rel, inner):
         share = shares[inner]
-        if rel:
-            wait(got_r.at[block, 1, pl.ds(0, share)], sem_r.at[block, 1])
-        else:
+        groups = GROUPS if rel else 1
+        size = share // groups
+        if not rel:
             part = got_r.at[block, 0, pl.ds(0, share), pl.ds(0, plane * TILE)]
             wait(part, sem_r.at[block, 0])
             if not inner:
@@ -218,18 +226,21 @@
             ).astype(jnp.bfloat16)
             return carry
 
-        lax.fori_loop(0, share, one, 0)
-        dst = got_t.at[block, rel, pl.ds(first_channel(inner, lane), share)]
-        for step in range(1, peers):
-            to = lax.rem(spot + step, peers)
-            remote(
-                tri.at[block, rel, pl.ds(0, share), pl.ds(to * rows, rows)], dst,
-                out_t.at[block, rel], sem_t.at[block, rel], half * peers + to,
-            )
-        pltpu.make_async_copy(
-            tri.at[block, rel, pl.ds(0, share), pl.ds(spot * rows, rows)], dst,
-            sem_t.at[block, rel],
-        ).start()
+        for group in range(groups):
+            channels = pl.ds(group * size, size)
+            if rel:
+                wait(got_r.at[block, 1, channels], sem_c.at[block, group])
+            lax.fori_loop(group * size, (group + 1) * size, one, 0)
+            dst = got_t.at[block, rel, pl.ds(first_channel(inner, lane) + group * size, size)]
+            for step in range(1, peers):
+                to = lax.rem(spot + step, peers)
+                remote(
+                    tri.at[block, rel, channels, pl.ds(to * rows, rows)], dst,
+                    out_t.at[block, rel], sem_t.at[block, rel], half * peers + to,
+                )
+            pltpu.make_async_copy(
+                tri.at[block, rel, channels, pl.ds(spot * rows, rows)], dst, sem_t.at[block, rel]
+            ).start()
 
     def finish(block, rel):
         pltpu.make_async_copy(
@@ -273,10 +284,16 @@
                 return carry
 
             lax.fori_loop(0, TILE, one_row, 0, unroll=2)
-
-    for block in range(blocks):
-        edges(block)
-        by_role(functools.partial(send_edges, block))
+        pltpu.make_async_copy(
+            out.at[:, devs, block], result.at[:, devs, block], sem_out.at[block, rel]
+        ).start()
+
+    for side in (1, 0):
+        for block in range(blocks):
+            edges(block, side)
+            if side and block == 0:
+                pl.semaphore_wait(barrier, n - 1)
+            by_role(functools.partial(send_edges, block, side))
 
     def ready(inner):
         for block in range(blocks):
@@ -306,6 +323,10 @@
                 )
 
     by_role(drain)
+    for block in range(blocks):
+        for rel in range(HALVES):
+            done = out.at[:, pl.ds(0, peers), block]
+            wait(done, sem_out.at[block, rel])
 
 
 def fused_body(n, pair_act, res_mask, w_left, w_right, w_gate, w_out):
@@ -315,15 +336,14 @@
     share = max(shares_of(width, peers))
     blocks = rows // TILE
     bf16 = jnp.bfloat16
-    wt = jnp.concatenate([w_left, w_right], axis=1).T
     view = (rows, n, blocks, TILE, depth)
     vmem = pl.BlockSpec(memory_space=pltpu.VMEM)
     dma = pltpu.SemaphoreType.DMA
     result = pl.pallas_call(
         functools.partial(kernel, n),
         out_shape=jax.ShapeDtypeStruct(view, bf16),
-        in_specs=[vmem, pl.BlockSpec(memory_space=pltpu.SMEM)] + [vmem] * 4,
-        out_specs=vmem,
+        in_specs=[vmem, pl.BlockSpec(memory_space=pltpu.SMEM)] + [vmem] * 5,
+        out_specs=pl.BlockSpec(memory_space=pl.ANY),
         scratch_shapes=[
             pltpu.VMEM(view, bf16),
             pltpu.VMEM((width, rows, length), bf16),
@@ -332,20 +352,24 @@
             pltpu.VMEM((blocks, HALVES, share, peers * TILE, length), bf16),
             pltpu.VMEM((blocks, HALVES, share, peers * rows, peers * TILE), bf16),
             pltpu.VMEM((blocks, HALVES, width, rows, peers * TILE), bf16),
-            pltpu.VMEM((length // LANES, 2, TILE * PITCH, LANES), jnp.float32),
+            pltpu.VMEM((length // LANES, TILE * PITCH, LANES), jnp.float32),
             pltpu.VMEM((width * FPITCH, LANES), jnp.float32),
+            pltpu.VMEM((2, 2 * width, depth), bf16),
+            pltpu.VMEM(view, bf16),
             dma,
             dma((blocks, 3)),
+            dma((blocks, GROUPS)),
             dma((blocks, HALVES)),
             dma,
             dma((blocks,)),
             dma((blocks,)),
             dma((blocks, HALVES)),
+            dma((blocks, HALVES)),
         ],
         compiler_params=pltpu.CompilerParams(
             collective_id=0, has_side_effects=True, vmem_limit_bytes=62 * 2**20
         ),
-    )(pair_act.reshape(view), res_mask, res_mask.reshape(1, length), wt, w_gate, w_out)
+    )(pair_act.reshape(view), res_mask, res_mask.reshape(1, length), w_left, w_right, w_gate, w_out)
     return result.reshape(rows, length, depth)
 
 

time: 249 us -> 238 us (0.956)
  Pallas kernels: 242 us -> 232 us
    pallas_call x1, Pallas kernels: 242 us -> 232 us  [fused_body(): pl.pallas_call(functools.partial(kernel, n), out_shape=jax.ShapeDtypeStru...]
    unnamed x3 -> x1, local copies, waits for them, and re-layouts: 6.56 us -> 4.65 us
where the time goes in v3:
time: 238 us; the launch traced here: 237 us
  Pallas kernels  232 us (97%)
  local copies, waits for them, and re-layouts  4.65 us (2%)
    pallas_call x1, Pallas kernels, fused_body(): pl.pallas_call(functools.partial(kernel, n), out_shape=jax.ShapeDtypeStru...  232 us

profile of v3, /device:TPU:7, one launch (start us, length us, event | category | flops | bytes accessed | tf_op | source)
XLA Modules:
  0.0 236.6 jit_solution(10059850896253979555)
XLA Ops:
  0.0 232.0 %shard_map.64 = bf16[32,16,2,16,128]{4,3,2,1,0:T(8,128)(2,1)} custom-call(bf16[32,16,2,16,128]{4,3,2,1,0:T(8,128)(2,1)} %bitcast.4, s32[512]{0:T(512)} %mask_s.1, s32[1,512]{1,0:T(1,128)} %bitcast.5, bf16[128,256]{1,0:T(8,128)(2,1)} %w_left.1, bf16[128,256]{1,0:T(8,128)(2,1)} %w_right.1, bf16[128,128]{1,0:T(8,128)(2,1)} %w_gate.1, bf16[128,128]{1,0:T(8,128)(2,1)} %w_out.1), custom_call_target="tpu_custom_call" | custom-call | tf_op jit(solution)/shard_map/pallas_call | solution.py:342
  232.0 4.7 %copy.8 = bf16[32,512,128]{2,1,0:T(8,128)(2,1)} copy(bf16[32,512,128]{2,1,0:T(8,128)(2,1)} %bitcast.3) | data formatting | bytes 8388608
